TPU v7x, 32 devices: a whole 2x2x4 slice. The times are simulated.
32 devices in a mesh: dp: 8 (over z, y), tensor: 4 (over x, core).
Axes of the slice: x: 2, y: 2, z: 4, core: 2. Of those that a mesh axis runs over, the one named last changes fastest.
Arguments:
- inputs: bfloat16 [16384, 1024], P(('dp', 'tensor')), may hold values from -6 to 6
- qkv_weight: bfloat16 [3, 1024, 1024], P(None, 'dp', 'tensor'), may hold values from -0.25 to 0.25
- qv_bias: bfloat16 [2, 1024], P(None, ('tensor', 'dp')), may hold values from -2 to 2
- proj_weight: bfloat16 [1024, 1024], P('tensor', 'dp'), may hold values from -0.5 to 0.5
- proj_bias: bfloat16 [1024], P('dp'), may hold values from -2 to 2
- fc_weight: bfloat16 [1024, 4096], P('dp', 'tensor'), may hold values from -0.1875 to 0.1875
- fc_bias: bfloat16 [4096], P(('tensor', 'dp')), may hold values from -2 to 2
- out_weight: bfloat16 [4096, 1024], P('tensor', 'dp'), may hold values from -0.1875 to 0.1875
- out_bias: bfloat16 [1024], P('dp'), may hold values from -2 to 2
- attn_norm_gain: bfloat16 [1024], P('dp'), may hold values from 0.5 to 1.5
- attn_norm_bias: bfloat16 [1024], P('dp'), may hold values from -2 to 2
- mlp_norm_gain: bfloat16 [1024], P('dp'), may hold values from 0.5 to 1.5
- mlp_norm_bias: bfloat16 [1024], P('dp'), may hold values from -2 to 2
- cotangent: bfloat16 [16384, 1024], P(('dp', 'tensor')), may hold values from -6 to 6
Outputs:
- outputs: bfloat16 [16384, 1024], P(('dp', 'tensor'))
- grad_inputs: bfloat16 [16384, 1024], P(('dp', 'tensor'))
- grad_qkv_weight: float32 [3, 1024, 1024], P(None, 'dp', 'tensor')
- grad_qv_bias: float32 [2, 1024], P(None, ('tensor', 'dp'))
- grad_proj_weight: float32 [1024, 1024], P('tensor', 'dp')
- grad_proj_bias: float32 [1024], P('dp')
- grad_fc_weight: float32 [1024, 4096], P('dp', 'tensor')
- grad_fc_bias: float32 [4096], P(('tensor', 'dp'))
- grad_out_weight: float32 [4096, 1024], P('tensor', 'dp')
- grad_out_bias: float32 [1024], P('dp')
- grad_attn_norm_gain: float32 [1024], P('dp')
- grad_attn_norm_bias: float32 [1024], P('dp')
- grad_mlp_norm_gain: float32 [1024], P('dp')
- grad_mlp_norm_bias: float32 [1024], P('dp')
All inputs are finite; a program needn't handle non-finite values.
Results may differ from a plain program's by a relative error of at most 0.02.
Values may be sent and summed in bfloat16 or wider, within the bound.
No kernel may reach another device: no remote copies, remote signals or barrier semaphores. Data moves between devices by JAX's collectives and lax.ppermute only.
A program may use at most 192 MiB of HBM per device.

v0:
```python
import math

import jax
import jax.numpy as jnp
from jax import lax
from jax.sharding import PartitionSpec as P

HD = 64


EPSILON = 1e-05
NEGATIVE = -1e30
ROOT_TWO_PI = 0.7978845608028654


def layer_norm(values, gain_vec, shift_vec):
    average = jnp.mean(values, axis=-1, keepdims=True)
    centered = values - average
    spread = jnp.mean(centered * centered, axis=-1, keepdims=True)
    return centered * lax.rsqrt(spread + EPSILON) * gain_vec + shift_vec


def gelu_tanh(values):
    return (
        0.5
        * values
        * (1.0 + jnp.tanh(ROOT_TWO_PI * (values + 0.044715 * values * values * values)))
    )


def masked_scores(queries, all_keys, offset):
    scaling = 1.0 / math.sqrt(queries.shape[2])
    scores = (
        jnp.einsum("qhd,khd->hqk", queries, all_keys, preferred_element_type=jnp.float32) * scaling
    )
    row_pos = offset + jnp.arange(queries.shape[0], dtype=jnp.int32)[:, None]
    col_pos = jnp.arange(all_keys.shape[0], dtype=jnp.int32)[None, :]
    return jnp.where(col_pos <= row_pos, scores, NEGATIVE)


def attend(queries, all_keys, all_values, block_rows):
    length, head_count, head_size = queries.shape

    def one_block(block_index):
        offset = block_index * block_rows
        query_rows = lax.dynamic_slice_in_dim(queries, offset, block_rows, 0)
        scores = masked_scores(query_rows, all_keys, offset)
        maximum = jnp.max(scores, axis=-1, keepdims=True)
        powers = jnp.exp(scores - maximum)
        totals = jnp.sum(powers, axis=-1, keepdims=True)
        weights = (powers / totals).astype(jnp.bfloat16)
        result = jnp.einsum("hqk,khd->qhd", weights, all_values, preferred_element_type=jnp.float32)
        return (result, (maximum + jnp.log(totals))[:, :, 0])

    results, log_totals = lax.map(one_block, jnp.arange(length // block_rows, dtype=jnp.int32))
    return (results.reshape(length, head_count * head_size).astype(jnp.bfloat16), log_totals)


def attend_back(queries, all_keys, all_values, log_totals, grad_mixed, block_rows):
    length, head_count, head_size = queries.shape
    scaling = 1.0 / math.sqrt(head_size)

    def one_block(running, block_index):
        key_grad, value_grad = running
        offset = block_index * block_rows
        query_rows = lax.dynamic_slice_in_dim(queries, offset, block_rows, 0)
        grad_rows = lax.dynamic_slice_in_dim(grad_mixed, offset, block_rows, 0)
        scores = masked_scores(query_rows, all_keys, offset)
        weights = jnp.exp(scores - log_totals[block_index][:, :, None])
        grad_weights = jnp.einsum(
            "qhd,khd->hqk", grad_rows, all_values, preferred_element_type=jnp.float32
        )
        inner_sum = jnp.sum(weights * grad_weights, axis=-1, keepdims=True)
        grad_scores = (weights * (grad_weights - inner_sum)).astype(jnp.bfloat16)
        query_grad = (
            jnp.einsum("hqk,khd->qhd", grad_scores, all_keys, preferred_element_type=jnp.float32)
            * scaling
        )
        key_grad = (
            key_grad
            + jnp.einsum(
                "hqk,qhd->khd", grad_scores, query_rows, preferred_element_type=jnp.float32
            )
            * scaling
        )
        value_grad = value_grad + jnp.einsum(
            "hqk,qhd->khd",
            weights.astype(jnp.bfloat16),
            grad_rows,
            preferred_element_type=jnp.float32,
        )
        return ((key_grad, value_grad), query_grad)

    zero_grads = jnp.zeros((length, head_count, head_size), jnp.float32)
    (key_grad, value_grad), query_grads = lax.scan(
        one_block, (zero_grads, zero_grads), jnp.arange(length // block_rows, dtype=jnp.int32)
    )
    width_all = head_count * head_size
    return (
        query_grads.reshape(length, width_all),
        key_grad.reshape(length, width_all),
        value_grad.reshape(length, width_all),
    )


def local(
    inputs,
    qkv_weight,
    qv_bias,
    proj_weight,
    proj_bias,
    fc_weight,
    fc_bias,
    out_weight,
    out_bias,
    attn_norm_gain,
    attn_norm_bias,
    mlp_norm_gain,
    mlp_norm_bias,
    cotangent,
):
    gathered = (
        lax.all_gather(qkv_weight, "dp", axis=1, tiled=True),
        lax.all_gather(qv_bias, "dp", axis=1, tiled=True),
        lax.all_gather(proj_weight, "dp", axis=1, tiled=True),
        lax.all_gather(fc_weight, "dp", axis=0, tiled=True),
        lax.all_gather(fc_bias, "dp", axis=0, tiled=True),
        lax.all_gather(out_weight, "dp", axis=1, tiled=True),
        lax.all_gather(proj_bias, "dp", axis=0, tiled=True),
        lax.all_gather(out_bias, "dp", axis=0, tiled=True),
        lax.all_gather(attn_norm_gain, "dp", axis=0, tiled=True),
        lax.all_gather(attn_norm_bias, "dp", axis=0, tiled=True),
        lax.all_gather(mlp_norm_gain, "dp", axis=0, tiled=True),
        lax.all_gather(mlp_norm_bias, "dp", axis=0, tiled=True),
    )
    qkv_full, qv_full, proj_full, fc_full, fc_bias_full, out_full = gathered[:6]
    proj_shift, out_shift, gain_one, shift_one, gain_two, shift_two = [
        member.astype(jnp.float32) for member in gathered[6:]
    ]
    local_width = qkv_full.shape[2]
    head_count = local_width // HD
    local_rows = inputs.shape[0]
    length = local_rows * lax.axis_size("tensor")
    block_rows = min(512, length)
    residual_in = inputs.astype(jnp.float32)
    normed_one = layer_norm(residual_in, gain_one, shift_one).astype(jnp.bfloat16)
    rows_one = lax.all_gather(normed_one, "tensor", axis=0, tiled=True)
    qv_shift = qv_full.astype(jnp.float32)
    biases = jnp.stack([qv_shift[0], jnp.zeros_like(qv_shift[0]), qv_shift[1]])
    projected = (
        jnp.einsum("sd,jde->jse", rows_one, qkv_full, preferred_element_type=jnp.float32)
        + biases[:, None, :]
    ).astype(jnp.bfloat16)
    shaped = projected.reshape(3, length, head_count, HD)
    mixed_heads, log_totals = attend(shaped[0], shaped[1], shaped[2], block_rows)
    residual = (
        residual_in
        + lax.psum_scatter(
            jnp.dot(mixed_heads, proj_full, preferred_element_type=jnp.float32).astype(
                jnp.bfloat16
            ),
            "tensor",
            scatter_dimension=0,
            tiled=True,
        ).astype(jnp.float32)
        + proj_shift
    )
    normed_two = layer_norm(residual, gain_two, shift_two).astype(jnp.bfloat16)
    rows_two = lax.all_gather(normed_two, "tensor", axis=0, tiled=True)
    hidden = jnp.dot(rows_two, fc_full, preferred_element_type=jnp.float32) + fc_bias_full.astype(
        jnp.float32
    )
    activated = gelu_tanh(hidden).astype(jnp.bfloat16)
    outputs = (
        residual
        + lax.psum_scatter(
            jnp.dot(activated, out_full, preferred_element_type=jnp.float32).astype(jnp.bfloat16),
            "tensor",
            scatter_dimension=0,
            tiled=True,
        ).astype(jnp.float32)
        + out_shift
    ).astype(jnp.bfloat16)
    grad_full = lax.all_gather(cotangent, "tensor", axis=0, tiled=True)
    grad_out_weight = jnp.einsum(
        "sf,sd->fd", activated, grad_full, preferred_element_type=jnp.float32
    )
    grad_act = jnp.einsum("sd,fd->sf", grad_full, out_full, preferred_element_type=jnp.float32)
    grad_hidden = jax.vjp(gelu_tanh, hidden)[1](grad_act)[0].astype(jnp.bfloat16)
    grad_fc_weight = jnp.einsum(
        "sd,sf->df", rows_two, grad_hidden, preferred_element_type=jnp.float32
    )
    grad_fc_bias = jnp.sum(grad_hidden.astype(jnp.float32), axis=0)
    grad_normed_two = lax.psum_scatter(
        jnp.einsum("sf,df->sd", grad_hidden, fc_full, preferred_element_type=jnp.float32).astype(
            jnp.bfloat16
        ),
        "tensor",
        scatter_dimension=0,
        tiled=True,
    ).astype(jnp.float32)
    grad_res_part, grad_gain_two, grad_shift_two = jax.vjp(
        layer_norm, residual, gain_two, shift_two
    )[1](grad_normed_two)
    grad_residual = cotangent.astype(jnp.float32) + grad_res_part
    branch_grad = grad_residual.astype(jnp.bfloat16)
    grad_proj_shift = jnp.sum(branch_grad.astype(jnp.float32), axis=0)
    branch_full = lax.all_gather(branch_grad, "tensor", axis=0, tiled=True)
    grad_proj_weight = jnp.einsum(
        "sk,sd->kd", mixed_heads, branch_full, preferred_element_type=jnp.float32
    )
    grad_mixed = jnp.einsum(
        "sd,kd->sk", branch_full, proj_full, preferred_element_type=jnp.float32
    ).astype(jnp.bfloat16)
    query_grad, key_grad, value_grad = attend_back(
        shaped[0],
        shaped[1],
        shaped[2],
        log_totals,
        grad_mixed.reshape(length, head_count, HD),
        block_rows,
    )
    grad_projected = jnp.stack([query_grad, key_grad, value_grad]).astype(jnp.bfloat16)
    grad_qv_bias = jnp.sum(grad_projected[0::2].astype(jnp.float32), axis=1)
    grad_qkv_weight = jnp.einsum(
        "sd,jse->jde", rows_one, grad_projected, preferred_element_type=jnp.float32
    )
    grad_normed_one = lax.psum_scatter(
        jnp.einsum(
            "jse,jde->sd", grad_projected, qkv_full, preferred_element_type=jnp.float32
        ).astype(jnp.bfloat16),
        "tensor",
        scatter_dimension=0,
        tiled=True,
    ).astype(jnp.float32)
    grad_in_part, grad_gain_one, grad_shift_one = jax.vjp(
        layer_norm, residual_in, gain_one, shift_one
    )[1](grad_normed_one)
    grad_inputs = (grad_residual + grad_in_part).astype(jnp.bfloat16)
    vector_grads = jnp.stack(
        [
            grad_proj_shift,
            jnp.sum(cotangent.astype(jnp.float32), axis=0),
            grad_gain_one,
            grad_shift_one,
            grad_gain_two,
            grad_shift_two,
        ]
    )
    vector_grads = lax.psum(vector_grads, "tensor")
    qkv_sum, qv_sum, proj_sum, fc_sum, fc_bias_sum, out_sum, vector_sum = (
        lax.psum_scatter(grad_qkv_weight, "dp", scatter_dimension=1, tiled=True),
        lax.psum_scatter(grad_qv_bias, "dp", scatter_dimension=1, tiled=True),
        lax.psum_scatter(grad_proj_weight, "dp", scatter_dimension=1, tiled=True),
        lax.psum_scatter(grad_fc_weight, "dp", scatter_dimension=0, tiled=True),
        lax.psum_scatter(grad_fc_bias, "dp", scatter_dimension=0, tiled=True),
        lax.psum_scatter(grad_out_weight, "dp", scatter_dimension=1, tiled=True),
        lax.psum_scatter(vector_grads, "dp", scatter_dimension=1, tiled=True),
    )
    return (
        outputs,
        grad_inputs,
        qkv_sum,
        qv_sum,
        proj_sum,
        vector_sum[0],
        fc_sum,
        fc_bias_sum,
        out_sum,
        vector_sum[1],
        vector_sum[2],
        vector_sum[3],
        vector_sum[4],
        vector_sum[5],
    )


def solution(mesh):
    return jax.shard_map(
        local,
        mesh=mesh,
        in_specs=(
            P(("dp", "tensor"), None),
            P(None, "dp", "tensor"),
            P(None, ("tensor", "dp")),
            P("tensor", "dp"),
            P("dp"),
            P("dp", "tensor"),
            P(("tensor", "dp")),
            P("tensor", "dp"),
            P("dp"),
            P("dp"),
            P("dp"),
            P("dp"),
            P("dp"),
            P(("dp", "tensor"), None),
        ),
        out_specs=(
            P(("dp", "tensor"), None),
            P(("dp", "tensor"), None),
            P(None, "dp", "tensor"),
            P(None, ("tensor", "dp")),
            P("tensor", "dp"),
            P("dp"),
            P("dp", "tensor"),
            P(("tensor", "dp")),
            P("tensor", "dp"),
            P("dp"),
            P("dp"),
            P("dp"),
            P("dp"),
            P("dp"),
        ),
        check_vma=False,
    )
```

profile of v0, /device:TPU:0, one launch (start us, length us, event | category | flops | bytes accessed | tf_op | source)
XLA Modules:
  0.0 1275.4 jit_solution(6162333602480248822)
XLA Ops:
  9.1 22.3 %all-gather = bf16[8,1,128]{2,1,0:T(2,128)(2,1)S(1)} all-gather(bf16[1,1,128]{2,1,0:T(2,128)(2,1)} %bitcast.185), channel_id=1, replica_groups=mesh['dp'=8,'tensor'=4] {'dp'}, dimensions={0}, use_global_device_ids=true | all-gather | bytes 2304 | tf_op jit(solution)/shard_map/all_gather | solution.py:131
  31.4 16.5 %all-gather.1 = bf16[8,1,128]{2,1,0:T(2,128)(2,1)S(1)} all-gather(bf16[1,1,128]{2,1,0:T(2,128)(2,1)} %bitcast.186), channel_id=1, replica_groups=mesh['dp'=8,'tensor'=4] {'dp'}, dimensions={0}, use_global_device_ids=true | all-gather | bytes 2304 | tf_op jit(solution)/shard_map/all_gather | solution.py:132
  53.8 18.0 %all-gather.2 = bf16[8,32,2]{1,2,0:T(2,128)(2,1)S(1)} all-gather(bf16[1,32,2]{1,2,0:T(2,128)(2,1)S(1)} %bitcast.187), channel_id=1, replica_groups=mesh['dp'=8,'tensor'=4] {'dp'}, dimensions={0}, use_global_device_ids=true | all-gather | bytes 1152 | tf_op jit(solution)/shard_map/all_gather | solution.py:124
  72.1 28.7 %all_gather.53 = bf16[256,1024]{1,0:T(8,128)(2,1)} all-gather(bf16[256,128]{1,0:T(8,128)(2,1)S(1)} %copy-done.25), channel_id=1, replica_groups=mesh['dp'=8,'tensor'=4] {'dp'}, dimensions={1}, use_global_device_ids=true | all-gather | bytes 589824 | tf_op jit(solution)/shard_map/all_gather | solution.py:125
  108.3 61.1 %while.27 = (s32[]{:T(128)}, bf16[4,512,4,64]{1,3,2,0:T(8,128)(2,1)}, f32[4,4,512]{2,1,0:T(4,128)}, s32[4]{0:T(128)S(1)}, bf16[2048,4,64]{0,2,1:T(8,128)(2,1)S(1...) while((s32[]{:T(128)}, ...), condition=%wide.region_5.6_spmd, body=%wide.region_2.5_spmd.sunk | while | flops 1125120512 | bytes 65868020 | solution.py:55
  177.5 16.2 %all-gather.3 = bf16[8,1,128]{2,1,0:T(2,128)(2,1)S(1)} all-gather(bf16[1,1,128]{2,1,0:T(2,128)(2,1)S(1)} %bitcast.188), channel_id=1, replica_groups=mesh['dp'=8,'tensor'=4] {'dp'}, dimensions={0}, use_global_device_ids=true | all-gather | bytes 2304 | tf_op jit(solution)/shard_map/all_gather | solution.py:129
  193.7 18.2 %all-gather.4 = bf16[8,1,128]{2,1,0:T(2,128)(2,1)S(1)} all-gather(bf16[1,1,128]{2,1,0:T(2,128)(2,1)S(1)} %bitcast.189), channel_id=1, replica_groups=mesh['dp'=8,'tensor'=4] {'dp'}, dimensions={0}, use_global_device_ids=true | all-gather | bytes 2304 | tf_op jit(solution)/shard_map/all_gather | solution.py:133
  211.8 16.2 %all-gather.5 = bf16[8,1,128]{2,1,0:T(2,128)(2,1)S(1)} all-gather(bf16[1,1,128]{2,1,0:T(2,128)(2,1)S(1)} %bitcast.190), channel_id=1, replica_groups=mesh['dp'=8,'tensor'=4] {'dp'}, dimensions={0}, use_global_device_ids=true | all-gather | bytes 2304 | tf_op jit(solution)/shard_map/all_gather | solution.py:134
  234.6 18.5 %all-gather.6 = bf16[8,1,128]{2,1,0:T(2,128)(2,1)S(1)} all-gather(bf16[1,1,128]{2,1,0:T(2,128)(2,1)S(1)} %bitcast.191), channel_id=1, replica_groups=mesh['dp'=8,'tensor'=4] {'dp'}, dimensions={0}, use_global_device_ids=true | all-gather | bytes 2304 | tf_op jit(solution)/shard_map/all_gather | solution.py:127
  253.1 17.8 %all-gather.22.cloned.1.call-done = bf16[1024,1024]{1,0:T(8,128)(2,1)} async-done(((bf16[128,1024]{1,0:T(8,128)(2,1)}), bf16[1024,1024]{1,0:T(8,128)(2,1)}) %all-gather.22.cloned.1.call-update) | async-done | bytes 2097168 | tf_op jit(solution)/shard_map/all_gather | solution.py:126
  270.9 35.1 %all-gather.20.cloned.1.call-done = bf16[2048,1024]{1,0:T(8,128)(2,1)} async-done(((bf16[512,1024]{1,0:T(8,128)(2,1)}), bf16[2048,1024]{1,0:T(8,128)(2,1)}) %all-gather.20.cloned.1.call-update) | async-done | bytes 4194320 | tf_op jit(solution)/shard_map/all_gather | solution.py:169
  316.6 42.5 %all-gather.24.cloned.1.call-done = bf16[1024,1024]{1,0:T(8,128)(2,1)} async-done(((bf16[1024,128]{1,0:T(8,128)(2,1)}), bf16[1024,1024]{1,0:T(8,128)(2,1)}) %all-gather.24.cloned.1.call-update) | async-done | bytes 2097168 | tf_op jit(solution)/shard_map/all_gather | solution.py:128
  359.2 34.3 %all-gather.26.cloned.1.call-done = bf16[2048,1024]{1,0:T(8,128)(2,1)} async-done(((bf16[512,1024]{1,0:T(8,128)(2,1)}), bf16[2048,1024]{1,0:T(8,128)(2,1)}) %all-gather.26.cloned.1.call-update) | async-done | bytes 4194320 | tf_op jit(solution)/shard_map/all_gather | solution.py:184
  393.5 15.6 %convert_reduce_fusion = (f32[1024]{0:T(1024)}, bf16[2048,1024]{1,0:T(8,128)(2,1)S(1)}) fusion(f32[2048,1024]{1,0:T(8,128)} %fusion.80, f32[1024]{0:T(1024)S(1)} %bitcast.182, bf16[2048,1024]{1,0:T(8,128)(2,1)} %all-gather.26.cloned.1.call-done, bf16[1024,1024]{1,0:T(8,128)(2,1)} %all-gather.24.cloned.1.call-done), kind=kOutput, calls=%fused_computation.56 | convolution fusion | flops 4351589376 | bytes 18882560 | tf_op jit(solution)/shard_map/sd,fd->sf/dot_general | solution.py:188
  417.8 11.7 convolution_convert_fusion.2
  430.1 20.4 %all-gather.7 = bf16[8,1,128]{2,1,0:T(2,128)(2,1)S(1)} all-gather(bf16[1,1,128]{2,1,0:T(2,128)(2,1)S(1)} %bitcast.192), channel_id=1, replica_groups=mesh['dp'=8,'tensor'=4] {'dp'}, dimensions={0}, use_global_device_ids=true | all-gather | bytes 2304 | tf_op jit(solution)/shard_map/all_gather | solution.py:130
  450.5 11.4 reduce-scatter.17.cloned.1.call-done
  464.8 44.2 %reduce-scatter.15.cloned.1.call-done = bf16[512,1024]{1,0:T(8,128)(2,1)} async-done(((bf16[2048,1024]{1,0:T(8,128)(2,1)}), bf16[512,1024]{1,0:T(8,128)(2,1)}) %reduce-scatter.15.cloned.1.call-update) | async-done | bytes 1048592 | tf_op jit(solution)/shard_map/reduce_scatter | solution.py:176
  516.1 34.6 %all-gather.28.cloned.1.call-done = bf16[2048,1024]{1,0:T(8,128)(2,1)} async-done(((bf16[512,1024]{1,0:T(8,128)(2,1)}), bf16[2048,1024]{1,0:T(8,128)(2,1)}) %all-gather.28.cloned.1.call-update) | async-done | bytes 4194320 | tf_op jit(solution)/shard_map/all_gather | solution.py:208
  556.3 198.7 %while.28 = (s32[]{:T(128)}, f32[2048,4,64]{0,2,1:T(8,128)}, f32[2048,4,64]{0,2,1:T(8,128)}, bf16[4,512,4,64]{1,3,2,0:T(8,128)(2,1)}, s32[4]{0:T(128)S(1)}, /*in...) while((s32[]{:T(128)}, f32[2048,4,64]{0,2,1:T(8,128)}, ...), condition=%wide.region_15.16_spmd.clone, body=%wide.region_13.15_spmd.clone.sunk | while | flops 2751068672 | bytes 180941136 | solution.py:95
  571.8 11.5 multiply_reduce_fusion.3
  621.0 11.5 multiply_reduce_fusion.3
  670.9 11.5 multiply_reduce_fusion.3
  720.7 11.5 multiply_reduce_fusion.3
  785.1 34.1 %reduce-scatter.19.cloned.1.call-done = bf16[512,1024]{1,0:T(8,128)(2,1)} async-done(((bf16[2048,1024]{1,0:T(8,128)(2,1)}), bf16[512,1024]{1,0:T(8,128)(2,1)}) %reduce-scatter.19.cloned.1.call-update) | async-done | bytes 1048592 | tf_op jit(solution)/shard_map/reduce_scatter | solution.py:228
  826.9 12.5 fusion.74
  856.5 21.4 %all-reduce = f32[1024]{0:T(1024)S(1)} all-reduce(f32[1024]{0:T(1024)S(1)} %copy-done.35), channel_id=11, replica_groups=mesh['dp'=8,'tensor'=4] {'dp'}, use_global_device_ids=true, to_apply=%region_33.34.clone | all-reduce | flops 1024 | bytes 8192
  885.2 76.5 %reduce-scatter.21.cloned.1.call-done = f32[3,128,256]{1,2,0:T(8,128)} async-done(((f32[3,1024,256]{1,2,0:T(8,128)}), f32[3,128,256]{1,2,0:T(8,128)}) %reduce-scatter.21.cloned.1.call-update) | async-done | bytes 393232 | tf_op jit(solution)/shard_map/reduce_scatter | solution.py:252
  963.6 53.7 %reduce-scatter.29.cloned.1.call-done = f32[6,128]{1,0:T(8,128)} async-done(((f32[6,1024]{1,0:T(8,128)}), f32[6,128]{1,0:T(8,128)}) %reduce-scatter.29.cloned.1.call-update) | async-done | bytes 3088 | tf_op jit(solution)/shard_map/reduce_scatter | solution.py:258
  1023.6 85.3 %reduce-scatter.27.cloned.1.call-done = f32[1024,128]{1,0:T(8,128)} async-done(((f32[1024,1024]{1,0:T(8,128)}), f32[1024,128]{1,0:T(8,128)}) %reduce-scatter.27.cloned.1.call-update) | async-done | bytes 524304 | tf_op jit(solution)/shard_map/reduce_scatter | solution.py:257
  1108.9 92.2 %reduce-scatter.25.cloned.1.call-done = f32[128,1024]{1,0:T(8,128)} async-done(((f32[1024,1024]{1,0:T(8,128)}), f32[128,1024]{1,0:T(8,128)}) %reduce-scatter.25.cloned.1.call-update) | async-done | bytes 524304 | tf_op jit(solution)/shard_map/reduce_scatter | solution.py:255
  1201.0 67.4 %reduce-scatter.23.cloned.1.call-done = f32[256,128]{1,0:T(8,128)} async-done(((f32[256,1024]{1,0:T(8,128)}), f32[256,128]{1,0:T(8,128)}) %reduce-scatter.23.cloned.1.call-update) | async-done | bytes 131088 | tf_op jit(solution)/shard_map/reduce_scatter | solution.py:254
  (288 shorter events, 334.9 us)
Async XLA Ops:
  7.2 46.6 %copy-start.38 = (bf16[2,32]{1,0:T(2,128)(2,1)S(1)}, bf16[2,32]{1,0:T(2,128)(2,1)}, u32[]{:S(2)}) copy-start(bf16[2,32]{1,0:T(2,128)(2,1)} %param.20) | copy-start | bytes 388
  7.2 64.9 %copy-start.25 = (bf16[256,128]{1,0:T(8,128)(2,1)S(1)}, bf16[256,128]{1,0:T(8,128)(2,1)}, u32[]{:S(2)}) copy-start(bf16[256,128]{1,0:T(8,128)(2,1)} %param.21) | copy-start | bytes 196612
  7.2 93.5 %all-gather.18.cloned.1.call-start = ((), (), s32[]{:S(2)}) async-start(), calls=%async_computation.11 | async-start | bytes 1769472 | tf_op jit(solution)/shard_map/all_gather | solution.py:123
  9.0 91.7 %all-gather.16.cloned.1.call-start = ((), (), s32[]{:S(2)}) async-start(), calls=%async_computation.10 | async-start | bytes 5242880 | tf_op jit(solution)/shard_map/all_gather | solution.py:147
  31.4 69.3 %copy-start.21 = (f32[8,1,128]{2,1,0:T(1,128)}, f32[8,1,128]{2,1,0:T(1,128)S(1)}, u32[]{:S(2)}) copy-start(f32[8,1,128]{2,1,0:T(1,128)S(1)} %convert_element_type.143) | copy-start | bytes 12292
  49.4 51.4 %copy-start.23 = (f32[512]{0:T(512)}, f32[512]{0:T(512)S(1)}, u32[]{:S(2)}) copy-start(f32[512]{0:T(512)S(1)} %broadcast_multiply_fusion.1) | copy-start | bytes 6148
  53.7 174.3 %reduce-scatter.13.cloned.1.call-start = ((), (), s32[]{:S(2)}) async-start(), calls=%async_computation.12 | async-start | bytes 5242880 | tf_op jit(solution)/shard_map/reduce_scatter | solution.py:158
  176.8 35.0 %copy-start.41 = (bf16[128]{0:T(256)(128)(2,1)S(1)}, bf16[128]{0:T(256)(128)(2,1)}, u32[]{:S(2)}) copy-start(bf16[128]{0:T(256)(128)(2,1)} %param.30) | copy-start | bytes 772
  176.8 51.2 %copy-start.2 = (bf16[512,1024]{1,0:T(8,128)(2,1)S(1)}, bf16[512,1024]{1,0:T(8,128)(2,1)}, u32[]{:S(2)}) copy-start(bf16[512,1024]{1,0:T(8,128)(2,1)} %param.18) | copy-start | bytes 3145732
  176.9 94.0 %all-gather.22.cloned.1.call-start = ((), (), s32[]{:S(2)}) async-start(), calls=%async_computation.14 | async-start | bytes 2359296 | tf_op jit(solution)/shard_map/all_gather | solution.py:126
  177.4 128.5 %all-gather.20.cloned.1.call-start = ((), (), s32[]{:S(2)}) async-start(), calls=%async_computation.13 | async-start | bytes 5242880 | tf_op jit(solution)/shard_map/all_gather | solution.py:169
  233.3 125.9 %all-gather.24.cloned.1.call-start = ((), (), s32[]{:S(2)}) async-start(), calls=%async_computation.15 | async-start | bytes 2359296 | tf_op jit(solution)/shard_map/all_gather | solution.py:128
  233.8 159.7 %all-gather.26.cloned.1.call-start = ((), (), s32[]{:S(2)}) async-start(), calls=%async_computation.17 | async-start | bytes 5242880 | tf_op jit(solution)/shard_map/all_gather | solution.py:184
  234.6 227.4 %reduce-scatter.17.cloned.1.call-start = ((), (), s32[]{:S(2)}) async-start(), calls=%async_computation.18 | async-start | bytes 5242880 | tf_op jit(solution)/shard_map/reduce_scatter | solution.py:194
  253.1 164.7 %copy-start.36 = (f32[8,1,128]{2,1,0:T(1,128)}, f32[8,1,128]{2,1,0:T(1,128)S(1)}, u32[]{:S(2)}) copy-start(f32[8,1,128]{2,1,0:T(1,128)S(1)} %convert_element_type.149) | copy-start | bytes 12292
  417.3 91.7 %reduce-scatter.15.cloned.1.call-start = ((), (), s32[]{:S(2)}) async-start(), calls=%async_computation.16 | async-start | bytes 5242880 | tf_op jit(solution)/shard_map/reduce_scatter | solution.py:176
  429.5 121.2 %all-gather.28.cloned.1.call-start = ((), (), s32[]{:S(2)}) async-start(), calls=%async_computation.19 | async-start | bytes 5242880 | tf_op jit(solution)/shard_map/all_gather | solution.py:208
  512.8 37.9 %copy-start.20 = (bf16[256,1024]{1,0:T(8,128)(2,1)S(1)}, bf16[256,1024]{1,0:T(8,128)(2,1)}, u32[]{:S(2)}) copy-start(bf16[256,1024]{1,0:T(8,128)(2,1)} %all_gather.53) | copy-start | bytes 1572868
  516.1 303.1 %reduce-scatter.19.cloned.1.call-start = ((), (), s32[]{:S(2)}) async-start(), calls=%async_computation.20 | async-start | bytes 5242880 | tf_op jit(solution)/shard_map/reduce_scatter | solution.py:228
  774.5 109.3 %reduce-scatter.31.cloned.1.call-start = ((), (), s32[]{:S(2)}) async-start(), calls=%async_computation.26 | async-start | bytes 147456
  777.2 42.0 %copy-start.3 = (bf16[512,1024]{1,0:T(8,128)(2,1)S(1)}, bf16[512,1024]{1,0:T(8,128)(2,1)}, u32[]{:S(2)}) copy-start(bf16[512,1024]{1,0:T(8,128)(2,1)} %param.18) | copy-start | bytes 3145732
  777.2 42.0 %copy-start.22 = (f32[8,1,128]{2,1,0:T(1,128)S(1)}, f32[8,1,128]{2,1,0:T(1,128)}, u32[]{:S(2)}) copy-start(f32[8,1,128]{2,1,0:T(1,128)} %copy-done.21) | copy-start | bytes 12292
  777.2 42.0 %copy-start.24 = (f32[512]{0:T(512)S(1)}, f32[512]{0:T(512)}, u32[]{:S(2)}) copy-start(f32[512]{0:T(512)} %copy-done.23) | copy-start | bytes 6148
  777.3 184.4 %reduce-scatter.21.cloned.1.call-start = ((), (), s32[]{:S(2)}) async-start(), calls=%async_computation.21 | async-start | bytes 3538944 | tf_op jit(solution)/shard_map/reduce_scatter | solution.py:252
  785.0 36.3 %copy-start.31 = (f32[512]{0:T(512)S(1)}, f32[512]{0:T(512)}, u32[]{:S(2)}) copy-start(f32[512]{0:T(512)} %copy-done.30) | copy-start | bytes 6148
  785.0 36.3 %copy-start.27 = (f32[512]{0:T(512)S(1)}, f32[512]{0:T(512)}, u32[]{:S(2)}) copy-start(f32[512]{0:T(512)} %copy-done.26) | copy-start | bytes 6148
  785.0 38.7 %copy-start.9 = (f32[512,1024]{1,0:T(8,128)S(1)}, f32[512,1024]{1,0:T(8,128)}, u32[]{:S(2)}) copy-start(f32[512,1024]{1,0:T(8,128)} %copy-done.8) | copy-start | bytes 6291460
  785.0 38.7 %copy-start.29 = (f32[512]{0:T(512)S(1)}, f32[512]{0:T(512)}, u32[]{:S(2)}) copy-start(f32[512]{0:T(512)} %copy-done.28) | copy-start | bytes 6148
  785.1 232.2 %reduce-scatter.29.cloned.1.call-start = ((), (), s32[]{:S(2)}) async-start(), calls=%async_computation.25 | async-start | bytes 36864 | tf_op jit(solution)/shard_map/reduce_scatter | solution.py:258
  826.6 282.3 %reduce-scatter.27.cloned.1.call-start = ((), (), s32[]{:S(2)}) async-start(), calls=%async_computation.24 | async-start | bytes 4718592 | tf_op jit(solution)/shard_map/reduce_scatter | solution.py:257
  839.4 361.6 %reduce-scatter.25.cloned.1.call-start = ((), (), s32[]{:S(2)}) async-start(), calls=%async_computation.23 | async-start | bytes 4718592 | tf_op jit(solution)/shard_map/reduce_scatter | solution.py:255
  849.6 418.9 %reduce-scatter.23.cloned.1.call-start = ((), (), s32[]{:S(2)}) async-start(), calls=%async_computation.22 | async-start | bytes 1179648 | tf_op jit(solution)/shard_map/reduce_scatter | solution.py:254
  (44 other events, 195.5 us)
Sparse Core Ops, SparseCore 0:
  10.7 48.0 all-gather.17
  60.9 32.6 all-gather.15
  177.0 42.3 reduce-scatter.12
  221.5 49.3 all-gather.21
  273.0 32.9 all-gather.19
  308.0 51.0 all-gather.23
  360.8 32.6 all-gather.25
  417.4 44.4 reduce-scatter.16
  464.5 44.4 reduce-scatter.14
  516.2 34.4 all-gather.27
  774.7 44.5 reduce-scatter.18
  823.0 60.8 reduce-scatter.30
  887.4 74.1 reduce-scatter.20
  964.6 52.6 reduce-scatter.28
  1021.4 87.4 reduce-scatter.26
  1113.4 87.6 reduce-scatter.24
  1204.9 63.5 reduce-scatter.22
where the time goes:
time: 1280 us
  waiting for transfers between devices  636 us (50%)
  matrix products  268 us (21%)
  blocking collectives  202 us (16%)
  other arithmetic  98 us (8%)
  local copies, waits for them, and re-layouts  40.2 us (3%)
  between operations  15.6 us (1%)
  loops' own time  13.9 us (1%)
    reduce_scatter x1, waiting for transfers between devices, local(): lax.psum_scatter(grad_fc_weight, 'dp', scatter_dimension=0, tiled=True)  92.2 us
    reduce_scatter x1, waiting for transfers between devices, local(): lax.psum_scatter(grad_out_weight, 'dp', scatter_dimension=1, tiled=True)  85.3 us
    reduce_scatter x1, waiting for transfers between devices, local(): lax.psum_scatter(grad_qkv_weight, 'dp', scatter_dimension=1, tiled=True)  76.5 us
    reduce_scatter x1, waiting for transfers between devices, local(): lax.psum_scatter(grad_proj_weight, 'dp', scatter_dimension=1, tiled=True)  67.4 us
    reduce_scatter x1, waiting for transfers between devices, local(): lax.psum_scatter(vector_grads, 'dp', scatter_dimension=1, tiled=True)  53.7 us
    dot_general x4, matrix products, one_block(): jnp.einsum('qhd,khd->hqk', grad_rows, all_values, preferred_element_type=...  46 us
    reduce_scatter x1, waiting for transfers between devices, local(): lax.psum_scatter(jnp.dot(activated, out_full, preferred_element_type=jnp....  44.2 us
    convert_element_type x4, other arithmetic, one_block(): grad_scores = (weights * (grad_weights - inner_sum)).astype(jnp.bfloat16)  44 us
  transfers between devices with their start and end apart: 17, of which 14 were waited for; matrix products, arithmetic and copies ran while one was open for 7% of the time, Pallas kernels for 0%

commit v1 on v0

v1 whole, which is shorter than its diff:
```python
import functools

import jax
import jax.numpy as jnp
from jax import lax
from jax.experimental import pallas as pl
from jax.experimental.pallas import tpu as pltpu
from jax.sharding import PartitionSpec as P

HD = 64
PAIR = 2 * HD
EPSILON = 1e-05
NEGATIVE = -1e30
ROOT_TWO_PI = 0.7978845608028654
F32 = jnp.float32
BF16 = jnp.bfloat16
VMEM_LIMIT = 40 * 1024 * 1024


def swap_x(value):
    return lax.ppermute(value, "tensor", [(0, 2), (2, 0), (1, 3), (3, 1)])


def swap_core(value):
    return lax.ppermute(value, "tensor", [(0, 1), (1, 0), (2, 3), (3, 2)])


def dot(a, b, contract, kind=F32):
    return lax.dot_general(a, b, (contract, ((), ())), preferred_element_type=kind)


NN = ((1,), (0,))
NT = ((1,), (1,))
TN = ((0,), (0,))


def normalize(values):
    average = jnp.mean(values, axis=-1, keepdims=True)
    centered = values - average
    spread = jnp.mean(centered * centered, axis=-1, keepdims=True)
    factor = lax.rsqrt(spread + EPSILON)
    return centered * factor, factor


def norm_back(unit, factor, gain, grad):
    scaled = grad * gain
    return factor * (
        scaled
        - jnp.mean(scaled, axis=-1, keepdims=True)
        - unit * jnp.mean(scaled * unit, axis=-1, keepdims=True)
    )


def gelu_both(values):
    squared = values * values
    bent = jnp.tanh(ROOT_TWO_PI * values * (1.0 + 0.044715 * squared))
    half = 0.5 * (1.0 + bent)
    slope = half + 0.5 * values * (1.0 - bent * bent) * ROOT_TWO_PI * (
        1.0 + 3.0 * 0.044715 * squared
    )
    return values * half, slope


def keep_head(block, which):
    lane = lax.broadcasted_iota(jnp.int32, block.shape, 1)
    return jnp.where((lane // HD) == which, block.astype(F32), 0.0).astype(BF16)


def attend_kernel(qkv_ref, mixed_ref, total_ref, peak, sums, acc, *, row0, block):
    count = mixed_ref.shape[0] // block
    lane = lax.broadcasted_iota(jnp.int32, (block, PAIR), 1)
    first = lane < HD
    causal = lax.broadcasted_iota(jnp.int32, (block, block), 1) <= lax.broadcasted_iota(
        jnp.int32, (block, block), 0
    )
    for i in range(count):
        start = row0 + i * block
        queries = qkv_ref[pl.ds(start, block), 0:PAIR].astype(F32) * (HD**-0.5)
        heads = [
            jnp.where(first, queries, 0.0).astype(BF16),
            jnp.where(first, 0.0, queries).astype(BF16),
        ]
        keys = qkv_ref[pl.ds(start, block), PAIR : 2 * PAIR]
        values = qkv_ref[pl.ds(start, block), 2 * PAIR : 3 * PAIR]
        for h in range(2):
            scores = jnp.where(causal, dot(heads[h], keys, NT), NEGATIVE)
            top = jnp.max(scores, axis=-1, keepdims=True)
            powers = jnp.exp(scores - top)
            peak[h] = top
            sums[h] = jnp.sum(powers, axis=-1, keepdims=True)
            acc[h] = dot(powers.astype(BF16), values, NN)

        def step(j, carry):
            at = pl.multiple_of(j * block, block)
            tile_keys = qkv_ref[pl.ds(at, block), PAIR : 2 * PAIR]
            tile_values = qkv_ref[pl.ds(at, block), 2 * PAIR : 3 * PAIR]
            for h in range(2):
                scores = dot(heads[h], tile_keys, NT)
                before = peak[h]
                top = jnp.maximum(before, jnp.max(scores, axis=-1, keepdims=True))
                shrink = jnp.exp(before - top)
                powers = jnp.exp(scores - top)
                peak[h] = top
                sums[h] = sums[h] * shrink + jnp.sum(powers, axis=-1, keepdims=True)
                acc[h] = acc[h] * shrink + dot(powers.astype(BF16), tile_values, NN)
            return carry

        if start:
            lax.fori_loop(0, start // block, step, 0)
        out = jnp.where(first, acc[0] / sums[0], acc[1] / sums[1])
        mixed_ref[i * block : (i + 1) * block, :] = out.astype(BF16)
        total_ref[i * block : (i + 1) * block, :] = jnp.where(
            first, peak[0] + jnp.log(sums[0]), peak[1] + jnp.log(sums[1])
        )


def attend(qkv, row0, rows, block):
    pairs = qkv.shape[1] // (3 * PAIR)
    return pl.pallas_call(
        functools.partial(attend_kernel, row0=row0, block=block),
        grid=(pairs,),
        in_specs=[pl.BlockSpec((row0 + rows, 3 * PAIR), lambda j: (0, j))],
        out_specs=[
            pl.BlockSpec((rows, PAIR), lambda j: (0, j)),
            pl.BlockSpec((rows, PAIR), lambda j: (0, j)),
        ],
        out_shape=[
            jax.ShapeDtypeStruct((rows, pairs * PAIR), BF16),
            jax.ShapeDtypeStruct((rows, pairs * PAIR), F32),
        ],
        scratch_shapes=[
            pltpu.VMEM((2, block, 1), F32),
            pltpu.VMEM((2, block, 1), F32),
            pltpu.VMEM((2, block, PAIR), F32),
        ],
        compiler_params=pltpu.CompilerParams(vmem_limit_bytes=VMEM_LIMIT),
        name="attend_%d" % row0,
    )(qkv)


def attend_back_kernel(
    qkv_ref, mixed_ref, grad_ref, total_ref, *rest, row0, block, has_before
):
    if has_before:
        before_ref, out_ref, key_acc, value_acc, query_acc = rest
    else:
        out_ref, key_acc, value_acc, query_acc = rest
    rows = mixed_ref.shape[0]
    count = rows // block
    lane = lax.broadcasted_iota(jnp.int32, (block, PAIR), 1)
    first = lane < HD
    causal = lax.broadcasted_iota(jnp.int32, (block, block), 0) <= lax.broadcasted_iota(
        jnp.int32, (block, block), 1
    )
    if has_before:
        key_acc[0:row0, :] = before_ref[:, PAIR : 2 * PAIR]
        value_acc[0:row0, :] = before_ref[:, 2 * PAIR : 3 * PAIR]
        key_acc[row0:, :] = jnp.zeros((rows, PAIR), F32)
        value_acc[row0:, :] = jnp.zeros((rows, PAIR), F32)
    else:
        key_acc[...] = jnp.zeros(key_acc.shape, F32)
        value_acc[...] = jnp.zeros(value_acc.shape, F32)
    for i in range(count):
        start = row0 + i * block
        local = slice(i * block, (i + 1) * block)
        queries = qkv_ref[pl.ds(start, block), 0:PAIR].astype(F32) * (HD**-0.5)
        grads = grad_ref[local, :].astype(F32)
        totals = jnp.transpose(total_ref[local, :])
        inner = jnp.transpose(grads * mixed_ref[local, :].astype(F32))
        query_heads, grad_heads, total_rows, inner_rows = [], [], [], []
        for h in range(2):
            mine = first if h == 0 else jnp.logical_not(first)
            query_heads.append(jnp.where(mine, queries, 0.0).astype(BF16))
            grad_heads.append(jnp.where(mine, grads, 0.0).astype(BF16))
            total_rows.append(totals[h * HD : h * HD + 1, :])
            inner_rows.append(jnp.sum(inner[h * HD : (h + 1) * HD, :], axis=0, keepdims=True))

        def tile(at, masked):
            tile_keys = qkv_ref[pl.ds(at, block), PAIR : 2 * PAIR]
            tile_values = qkv_ref[pl.ds(at, block), 2 * PAIR : 3 * PAIR]
            key_sum, value_sum = None, None
            for h in range(2):
                scores = dot(tile_keys, query_heads[h], NT)
                weights = jnp.exp(scores - total_rows[h])
                if masked:
                    weights = jnp.where(causal, weights, 0.0)
                grad_weights = dot(tile_values, grad_heads[h], NT)
                grad_scores = (weights * (grad_weights - inner_rows[h])).astype(BF16)
                value_part = dot(weights.astype(BF16), grad_heads[h], NN)
                key_part = dot(grad_scores, query_heads[h], NN)
                query_part = dot(grad_scores, tile_keys, TN)
                key_sum = key_part if key_sum is None else key_sum + key_part
                value_sum = value_part if value_sum is None else value_sum + value_part
                if masked:
                    query_acc[h] = query_part
                else:
                    query_acc[h] += query_part
            key_acc[pl.ds(at, block), :] += key_sum
            value_acc[pl.ds(at, block), :] += value_sum

        tile(start, True)

        def step(j, carry):
            tile(pl.multiple_of(j * block, block), False)
            return carry

        if start:
            lax.fori_loop(0, start // block, step, 0)
        query_grad = jnp.where(first, query_acc[0], query_acc[1]) * (HD**-0.5)
        out_ref[start : start + block, 0:PAIR] = query_grad.astype(out_ref.dtype)
    if has_before:
        out_ref[0:row0, 0:PAIR] = before_ref[:, 0:PAIR].astype(out_ref.dtype)
    out_ref[:, PAIR : 2 * PAIR] = key_acc[...].astype(out_ref.dtype)
    out_ref[:, 2 * PAIR : 3 * PAIR] = value_acc[...].astype(out_ref.dtype)


def attend_back(qkv, mixed, grads, totals, before, row0, block):
    pairs = qkv.shape[1] // (3 * PAIR)
    rows = mixed.shape[0]
    extent = row0 + rows
    narrow = pl.BlockSpec((rows, PAIR), lambda j: (0, j))
    in_specs = [pl.BlockSpec((extent, 3 * PAIR), lambda j: (0, j)), narrow, narrow, narrow]
    operands = [qkv, mixed, grads, totals]
    if before is not None:
        in_specs.append(pl.BlockSpec((row0, 3 * PAIR), lambda j: (0, j)))
        operands.append(before)
    return pl.pallas_call(
        functools.partial(
            attend_back_kernel, row0=row0, block=block, has_before=before is not None
        ),
        grid=(pairs,),
        in_specs=in_specs,
        out_specs=pl.BlockSpec((extent, 3 * PAIR), lambda j: (0, j)),
        out_shape=jax.ShapeDtypeStruct(
            (extent, pairs * 3 * PAIR), F32 if before is None else BF16
        ),
        scratch_shapes=[
            pltpu.VMEM((extent, PAIR), F32),
            pltpu.VMEM((extent, PAIR), F32),
            pltpu.VMEM((2, block, PAIR), F32),
        ],
        compiler_params=pltpu.CompilerParams(vmem_limit_bytes=VMEM_LIMIT),
        name="attend_back_%d" % row0,
    )(*operands)


def local(
    inputs,
    qkv_weight,
    qv_bias,
    proj_weight,
    proj_bias,
    fc_weight,
    fc_bias,
    out_weight,
    out_bias,
    attn_norm_gain,
    attn_norm_bias,
    mlp_norm_gain,
    mlp_norm_bias,
    cotangent,
):
    width = inputs.shape[1]
    rows = inputs.shape[0]
    share = proj_bias.shape[0]
    parts = width // share
    head_cols = qkv_weight.shape[2]
    pairs = head_cols // PAIR
    qkv_cols = 3 * head_cols
    hidden_cols = fc_weight.shape[1]
    place = lax.axis_index("tensor")
    core = place % 2
    is_low = place < 2
    is_first = core == 0

    def pick_x(low, high):
        return jnp.where(is_low, low, high)

    qv_column = jnp.pad(qv_bias.reshape(-1), (0, share - qv_bias.size))
    vectors = jnp.stack(
        [
            proj_bias,
            out_bias,
            attn_norm_gain,
            attn_norm_bias,
            mlp_norm_gain,
            mlp_norm_bias,
            fc_bias,
            qv_column,
        ],
        axis=1,
    )
    qkv_shard = jnp.transpose(
        qkv_weight.reshape(3, share, pairs, PAIR), (1, 2, 0, 3)
    ).reshape(share, qkv_cols)
    attn_shard = jnp.concatenate(
        [qkv_shard, proj_weight.T, jnp.pad(vectors, ((0, 0), (0, 120)))], axis=1
    )
    attn_all = lax.all_gather(attn_shard, "dp", axis=0, tiled=True)
    mlp_shard = jnp.concatenate([fc_weight, out_weight.T], axis=1)
    mlp_all = lax.all_gather(mlp_shard, "dp", axis=0, tiled=True)

    input_x = swap_x(inputs)
    input_core = swap_core(inputs)
    input_far = swap_core(input_x)
    input_low, input_high = pick_x(inputs, input_x), pick_x(input_x, inputs)
    far_low, far_high = pick_x(input_core, input_far), pick_x(input_far, input_core)
    cot_x = swap_x(cotangent)
    cots = [pick_x(cotangent, cot_x), pick_x(cot_x, cotangent)]
    sequence = jnp.concatenate(
        [
            jnp.where(is_first, input_low, far_low),
            jnp.where(is_first, far_low, input_low),
            jnp.where(is_first, input_high, far_high),
            jnp.where(is_first, far_high, input_high),
        ],
        axis=0,
    )

    attn_sib = swap_core(attn_all)
    columns = attn_all[:, qkv_cols + head_cols : qkv_cols + head_cols + 8].astype(F32).T
    proj_shift, out_shift, gain_one, shift_one, gain_two, shift_two = [
        columns[i][None, :] for i in range(6)
    ]
    fc_shift = jnp.concatenate(
        [columns[6], attn_sib[:, qkv_cols + head_cols + 6].astype(F32)], axis=0
    )[None, :]
    qv_shift = (
        columns[7]
        .reshape(parts, share)[:, : share // 2]
        .reshape(parts, 2, share // 4)
        .transpose(1, 0, 2)
        .reshape(2, head_cols)
    )
    qkv_shift = jnp.stack([qv_shift[0], jnp.zeros_like(qv_shift[0]), qv_shift[1]])
    qkv_shift = qkv_shift.reshape(3, pairs, PAIR).transpose(1, 0, 2).reshape(1, qkv_cols)
    proj_both = jnp.concatenate(
        [
            attn_all[:, qkv_cols : qkv_cols + head_cols],
            attn_sib[:, qkv_cols : qkv_cols + head_cols],
        ],
        axis=1,
    )

    normed_one = (normalize(sequence.astype(F32))[0] * gain_one + shift_one).astype(BF16)
    qkv = (dot(normed_one, attn_all[:, :qkv_cols], NN) + qkv_shift).astype(BF16)

    mlp_sib = swap_core(mlp_all)
    fc_both = jnp.concatenate([mlp_all[:, :hidden_cols], mlp_sib[:, :hidden_cols]], axis=1)
    out_both = jnp.concatenate([mlp_all[:, hidden_cols:], mlp_sib[:, hidden_cols:]], axis=1)

    inputs_two = [input_low, input_high]
    mixed, totals = [], []
    mixed_rows, units, factors, normed_two, acts, grads_hidden = [], [], [], [], [], []
    residuals, out_parts = [], []
    grad_residuals, branches, grad_mixed = [], [], []
    for half in range(2):
        half_mixed, half_totals = attend(qkv, half * 2 * rows, 2 * rows, rows)
        mixed.append(half_mixed)
        totals.append(half_totals)
        two = half_mixed.reshape(2, rows, head_cols)
        mine = jnp.where(is_first, two[0], two[1])
        received = swap_core(jnp.where(is_first, two[1], two[0]))
        both = jnp.concatenate([mine, received], axis=1)
        mixed_rows.append(both)
        part = dot(both, proj_both, NT).astype(BF16)
        residual = (
            inputs_two[half].astype(F32) + part.astype(F32) + swap_x(part).astype(F32) + proj_shift
        )
        residuals.append(residual)
    for half in range(2):
        unit, factor = normalize(residuals[half])
        units.append(unit)
        factors.append(factor)
        normed = (unit * gain_two + shift_two).astype(BF16)
        normed_two.append(normed)
        grad_act = dot(cots[half], out_both, NN).astype(BF16)
        hidden = dot(normed, fc_both, NN) + fc_shift
        act, slope = gelu_both(hidden)
        act = act.astype(BF16)
        grad_hidden = (grad_act.astype(F32) * slope).astype(BF16)
        acts.append(act)
        grads_hidden.append(grad_hidden)
        grad_part = dot(grad_hidden, fc_both, NT).astype(BF16)
        grad_normed = grad_part.astype(F32) + swap_x(grad_part).astype(F32)
        out_parts.append(dot(act, out_both, NT).astype(BF16))
        grad_residual = cots[half].astype(F32) + norm_back(unit, factor, gain_two, grad_normed)
        grad_residuals.append(grad_residual)
        branch = grad_residual.astype(BF16)
        branches.append(branch)
        grad_both = dot(branch, proj_both, NN).astype(BF16)
        mine = grad_both[:, :head_cols]
        received = swap_core(grad_both[:, head_cols:])
        grad_mixed.append(
            jnp.concatenate(
                [jnp.where(is_first, mine, received), jnp.where(is_first, received, mine)], axis=0
            )
        )
        if half == 0:
            vec_two = 0.0
        vec_two = vec_two + jnp.stack(
            [
                jnp.sum(branch.astype(F32), axis=0),
                jnp.sum(cots[half].astype(F32), axis=0),
                jnp.sum(grad_normed * unit, axis=0),
                jnp.sum(grad_normed, axis=0),
            ]
        )

    out_recv = swap_x(pick_x(out_parts[1], out_parts[0]))
    out_mine = pick_x(out_parts[0], out_parts[1])
    outputs = (
        pick_x(residuals[0], residuals[1])
        + out_mine.astype(F32)
        + out_recv.astype(F32)
        + out_shift
    ).astype(BF16)

    act_all = jnp.concatenate(acts, axis=0)
    grad_hidden_all = jnp.concatenate(grads_hidden, axis=0)
    normed_two_all = jnp.concatenate(normed_two, axis=0)
    cot_all = jnp.concatenate(cots, axis=0)
    fc_own = dot(normed_two_all, grad_hidden_all[:, :hidden_cols], TN)
    fc_sib = dot(normed_two_all, grad_hidden_all[:, hidden_cols:], TN).astype(BF16)
    out_own = dot(cot_all, act_all[:, :hidden_cols], TN)
    out_sib = dot(cot_all, act_all[:, hidden_cols:], TN).astype(BF16)
    fc_bias_sums = jnp.sum(grad_hidden_all.astype(F32), axis=0)
    grad_mlp = jnp.concatenate(
        [
            (fc_own + swap_core(fc_sib).astype(F32)).astype(BF16),
            (out_own + swap_core(out_sib).astype(F32)).astype(BF16),
        ],
        axis=1,
    )
    mlp_sum = lax.psum_scatter(grad_mlp, "dp", scatter_dimension=0, tiled=True)

    before = attend_back(qkv, mixed[0], grad_mixed[0], totals[0], None, 0, rows)
    grad_qkv = attend_back(qkv, mixed[1], grad_mixed[1], totals[1], before, 2 * rows, rows)

    branch_all = jnp.concatenate(branches, axis=0)
    mixed_all = jnp.concatenate(mixed_rows, axis=0)
    proj_grad = dot(branch_all, mixed_all, TN)
    proj_grad = proj_grad[:, :head_cols] + swap_core(
        proj_grad[:, head_cols:].astype(BF16)
    ).astype(F32)

    blocks = grad_qkv.reshape(2, 2, rows, qkv_cols)
    block_mine = jnp.where(is_first, blocks[:, 0], blocks[:, 1]).reshape(2 * rows, qkv_cols)
    block_sent = jnp.where(is_first, blocks[:, 1], blocks[:, 0]).reshape(2 * rows, qkv_cols)
    block_recv = swap_core(block_sent)
    z_part = dot(block_mine, attn_all[:, :qkv_cols], NT) + dot(
        block_recv, attn_sib[:, :qkv_cols], NT
    )
    z_low, z_high = z_part[:rows], z_part[rows:]
    z_recv = swap_x(pick_x(z_high, z_low).astype(BF16))
    unit_low, factor_low = normalize(input_low.astype(F32))
    unit_high, factor_high = normalize(input_high.astype(F32))
    vec_one = jnp.stack(
        [
            jnp.sum(z_low * unit_low, axis=0) + jnp.sum(z_high * unit_high, axis=0),
            jnp.sum(z_low, axis=0) + jnp.sum(z_high, axis=0),
        ]
    )
    qkv_grad = dot(normed_one, grad_qkv, TN)
    bias_sums = jnp.sum(grad_qkv.astype(F32), axis=0).reshape(pairs, 3, PAIR)
    qv_sums = jnp.stack([bias_sums[:, 0].reshape(-1), bias_sums[:, 2].reshape(-1)])
    qv_sums = qv_sums.reshape(2, parts, share // 4).transpose(1, 0, 2).reshape(parts, share // 2)
    qv_sums = jnp.pad(qv_sums, ((0, 0), (0, share - share // 2))).reshape(-1)
    fc_bias_grad = fc_bias_sums[:hidden_cols] + swap_core(fc_bias_sums[hidden_cols:])
    vec_grads = jnp.concatenate(
        [0.5 * vec_two[:2], vec_one, 0.5 * vec_two[2:], fc_bias_grad[None], qv_sums[None]], axis=0
    ).T
    grad_attn = jnp.concatenate(
        [
            qkv_grad.astype(BF16),
            proj_grad.astype(BF16),
            jnp.pad(vec_grads, ((0, 0), (0, 120))).astype(BF16),
        ],
        axis=1,
    )
    attn_sum = lax.psum_scatter(grad_attn, "dp", scatter_dimension=0, tiled=True)

    unit = pick_x(unit_low, unit_high)
    factor = pick_x(factor_low, factor_high)
    z_own = pick_x(z_low, z_high) + z_recv.astype(F32)
    grad_inputs = (
        pick_x(grad_residuals[0], grad_residuals[1]) + norm_back(unit, factor, gain_one, z_own)
    ).astype(BF16)

    qkv_out = (
        attn_sum[:, :qkv_cols]
        .astype(F32)
        .reshape(share, pairs, 3, PAIR)
        .transpose(2, 0, 1, 3)
        .reshape(3, share, head_cols)
    )
    proj_out = attn_sum[:, qkv_cols : qkv_cols + head_cols].astype(F32).T
    sums = attn_sum[:, qkv_cols + head_cols : qkv_cols + head_cols + 8].astype(F32).T
    six = lax.psum(sums[:6], "tensor")
    qv_out = sums[7][: share // 2].reshape(2, share // 4)
    fc_out = mlp_sum[:, :hidden_cols].astype(F32)
    out_out = mlp_sum[:, hidden_cols:].astype(F32).T
    return (
        outputs,
        grad_inputs,
        qkv_out,
        qv_out,
        proj_out,
        six[0],
        fc_out,
        sums[6],
        out_out,
        six[1],
        six[2],
        six[3],
        six[4],
        six[5],
    )


def solution(mesh):
    rows = P(("dp", "tensor"), None)
    vector = P("dp")
    wide = P(("tensor", "dp"))
    weights = (
        P(None, "dp", "tensor"),
        P(None, ("tensor", "dp")),
        P("tensor", "dp"),
        vector,
        P("dp", "tensor"),
        wide,
        P("tensor", "dp"),
        vector,
        vector,
        vector,
        vector,
        vector,
    )
    return jax.shard_map(
        local,
        mesh=mesh,
        in_specs=(rows, *weights, rows),
        out_specs=(rows, rows, *weights),
        check_vma=False,
    )
```

time: 1280 us -> 578 us (0.45)
  waiting for transfers between devices: 636 us -> 292 us
  blocking collectives: 202 us -> 5.63 us
  matrix products: 268 us -> 77.4 us
  Pallas kernels: 0 us -> 78.3 us
  other arithmetic: 98 us -> 48.2 us
  starting transfers between devices: 1.35 us -> 15.4 us
  loops' own time: 13.9 us -> 0 us
    reduce_scatter x9 -> x0, waiting for transfers between devices: 465 us -> none  [the longest x1 92.2 us: local(): lax.psum_scatter(grad_fc_weight, 'dp', scatter_dimension=0, tiled=True)]
    dot_general x40 -> x21, matrix products: 268 us -> 77.4 us  [dot(): lax.dot_general(a, b, (contract, ((), ())), preferred_element_type=kind)]
    all_gather x9 -> x0, blocking collectives: 175 us -> none  [the longest x1 28.7 us: local(): lax.all_gather(proj_weight, 'dp', axis=1, tiled=True)]
    ppermute x0 -> x21, waiting for transfers between devices: none -> 133 us  [the longest x8 127 us: swap_x(): return lax.ppermute(value, 'tensor', [(0, 2), (2, 0), (1, 3), (3, 1)])]
    all_gather x7 -> x2, waiting for transfers between devices: 164 us -> 38.6 us  [the longest x1 20.8 us: local(): mlp_all = lax.all_gather(mlp_shard, 'dp', axis=0, tiled=True)]
    unnamed x18 -> x6, waiting for transfers between devices: 7.37 us -> 120 us
    pallas_call x0 -> x4, Pallas kernels: none -> 78.3 us  [the longest x2 41.8 us: attend(): pl.pallas_call(functools.partial(attend_kernel, row0=row0, block=block),...]
    convert_element_type x14 -> x5, other arithmetic: 48.3 us -> 7.65 us  [the longest x1 3.62 us: local(): grad_inputs = (pick_x(grad_residuals[0], grad_residuals[1]) + norm_back(u...]
  transfers between devices with their start and end apart: 17 -> 25, of which waited for: 14 -> 15; matrix products, arithmetic and copies ran while one was open for 7% -> 18% of each run, Pallas kernels for 0% -> 9%
where the time goes in v1:
time: 578 us; the launch traced here: 568 us
  waiting for transfers between devices  292 us (51%)
  Pallas kernels  78.3 us (14%)
  matrix products  77.4 us (13%)
  other arithmetic  48.2 us (8%)
  local copies, waits for them, and re-layouts  36.4 us (6%)
  starting transfers between devices  15.4 us (3%)
  between operations  15.3 us (3%)
    ppermute x8, waiting for transfers between devices, swap_x(): return lax.ppermute(value, 'tensor', [(0, 2), (2, 0), (1, 3), (3, 1)])  127 us
    unnamed x6, waiting for transfers between devices  120 us
    dot_general x21, matrix products, dot(): lax.dot_general(a, b, (contract, ((), ())), preferred_element_type=kind)  77.4 us
    pallas_call x2, Pallas kernels, attend(): pl.pallas_call(functools.partial(attend_kernel, row0=row0, block=block),...  41.8 us
    pallas_call x2, Pallas kernels, attend_back(): pl.pallas_call(functools.partial(attend_back_kernel, row0=row0, block=blo...  36.5 us
    unnamed x118, local copies, waits for them, and re-layouts  25.9 us
    all_gather x1, waiting for transfers between devices, local(): mlp_all = lax.all_gather(mlp_shard, 'dp', axis=0, tiled=True)  20.8 us
    all_gather x1, waiting for transfers between devices, local(): attn_all = lax.all_gather(attn_shard, 'dp', axis=0, tiled=True)  17.8 us
  transfers between devices with their start and end apart: 25, of which 15 were waited for; matrix products, arithmetic and copies ran while one was open for 18% of the time, Pallas kernels for 9%

profile of v1, /device:TPU:0, one launch (start us, length us, event | category | flops | bytes accessed | tf_op | source)
XLA Modules:
  0.0 568.4 jit_solution(4494357825665476966)
XLA Ops:
  13.7 3.0 collective-permute-start
  16.7 23.2 %collective-permute-done = bf16[512,1024]{1,0:T(8,128)(2,1)S(1)} collective-permute-done((bf16[512,1024]{1,0:T(8,128)(2,1)S(1)}, bf16[512,1024]{1,0:T(8,128)(2,1)S(1)}, u32[]{:S(2)}, u32[]{:S(2)}) %collective-permute-start) | collective-permute-done | bytes 1048608 | tf_op jit(solution)/shard_map/ppermute | solution.py:21
  46.8 3.5 fusion.2
  50.3 17.8 %all-gather.3.cloned.1.call-done = bf16[1024,1152]{0,1:T(8,128)(2,1)} async-done(((bf16[128,1152]{0,1:T(8,128)(2,1)}), bf16[1024,1152]{0,1:T(8,128)(2,1)}) %all-gather.3.cloned.1.call-update) | async-done | bytes 2359312 | tf_op jit(solution)/shard_map/all_gather | solution.py:299
  69.3 8.6 %add_convert_fusion.qkv_ref = bf16[2048,768]{1,0:T(8,128)(2,1)S(1)} fusion(f32[768]{0:T(1024)S(1)} %add.253, bf16[1024,1152]{0,1:T(8,128)(2,1)} %all-gather.3.cloned.1.call-done, f32[1024]{0:T(1024)S(1)} %bitcast.124, f32[1024]{0:T(1024)S(1)} %bitcast.106, f32[2048]{0:T(1024)S(1)} %add_rsqrt_fusion, f32[2048]{0:T(1024)S(1)} %broadcast_multiply_fusion, ...), kind=kOutput, calls=%fused_computation.9 | convolution fusion | flops 3251634176 | bytes 8940544 | tf_op jit(solution)/shard_map/dot_general | solution.py:29
  77.9 11.7 %attend_0.1 = (bf16[1024,256]{1,0:T(8,128)(2,1)S(1)}, f32[1024,256]{1,0:T(8,128)S(1)}) custom-call(bf16[2048,768]{1,0:T(8,128)(2,1)S(1)} %add_convert_fusion.qkv_ref), custom_call_target="tpu_custom_call" | custom-call | tf_op jit(solution)/shard_map/attend_0/pallas_call | solution.py:119
  91.4 30.1 %attend_1024.1 = (bf16[1024,256]{1,0:T(8,128)(2,1)S(1)}, f32[1024,256]{1,0:T(8,128)S(1)}) custom-call(bf16[2048,768]{1,0:T(8,128)(2,1)S(1)} %add_convert_fusion.qkv_ref), custom_call_target="tpu_custom_call" | custom-call | tf_op jit(solution)/shard_map/attend_1024/pallas_call | solution.py:119
  123.3 20.8 %all-gather.5.cloned.1.call-done = bf16[1024,2048]{0,1:T(8,128)(2,1)} async-done(((bf16[128,2048]{0,1:T(8,128)(2,1)}), bf16[1024,2048]{0,1:T(8,128)(2,1)}) %all-gather.5.cloned.1.call-update) | async-done | bytes 4194320 | tf_op jit(solution)/shard_map/all_gather | solution.py:301
  160.3 18.7 %collective-permute-done.5 = bf16[512,1024]{1,0:T(8,128)(2,1)S(1)} collective-permute-done((bf16[512,1024]{1,0:T(8,128)(2,1)S(1)}, bf16[512,1024]{1,0:T(8,128)(2,1)S(1)}, u32[]{:S(2)}, u32[]{:S(2)}) %collective-permute-start.5) | collective-permute-done | bytes 1048608 | tf_op jit(solution)/shard_map/ppermute | solution.py:21
  179.1 21.7 %collective-permute-done.7 = bf16[512,1024]{1,0:T(8,128)(2,1)S(1)} collective-permute-done((bf16[512,1024]{1,0:T(8,128)(2,1)S(1)}, bf16[512,1024]{1,0:T(8,128)(2,1)S(1)}, u32[]{:S(2)}, u32[]{:S(2)}) %collective-permute-start.7) | collective-permute-done | bytes 1048608 | tf_op jit(solution)/shard_map/ppermute | solution.py:21
  205.1 4.3 fusion.82
  209.5 9.8 %multiply_convert_fusion.3 = (bf16[512,2048]{1,0:T(8,128)(2,1)S(1)}, bf16[512,2048]{1,0:T(8,128)(2,1)S(1)}, f32[512,2048]{1,0:T(8,128)}) fusion(f32[2048]{0:T(1024)S(1)} %pad_maximum_fusion.19, f32[512,2048]{1,0:T(8,128)} %fusion.82, bf16[512,1024]{1,0:T(8,128)(2,1)S(1)} %get-tuple-element.160, bf16[1024,1024]{0,1:T(8,128)(2,1)S(1)} %get-tuple-element.118, ...), kind=kOutput, calls=%fused_computation.30 | convolution fusion | flops 2176843776 | bytes 17833984 | tf_op jit(solution)/shard_map/dot_general | solution.py:29
  219.3 9.9 %multiply_convert_fusion = bf16[512,2048]{1,0:T(8,128)(2,1)S(1)} fusion(f32[512,2048]{1,0:T(8,128)} %fusion.82, f32[2048]{0:T(1024)S(1)} %pad_maximum_fusion.19, bf16[512,1024]{1,0:T(8,128)(2,1)S(1)} %get-tuple-element.131, bf16[1024,1024]{0,1:T(8,128)(2,1)S(1)} %get-tuple-element.117, bf16[1024,1024]{0,1:T(8,128)(2,1)S(1)} %get-tuple-element.115), kind=kOutput, calls=%fused_computation.25 | convolution fusion | flops 2177892352 | bytes 11542528 | tf_op jit(solution)/shard_map/dot_general | solution.py:29
  233.1 8.6 %multiply_convert_fusion.1 = bf16[512,2048]{1,0:T(8,128)(2,1)S(1)} fusion(f32[512,2048]{1,0:T(8,128)} %get-tuple-element.174, f32[2048]{0:T(1024)S(1)} %pad_maximum_fusion.19, bf16[512,1024]{1,0:T(8,128)(2,1)S(1)} %get-tuple-element.105, bf16[1024,1024]{0,1:T(8,128)(2,1)S(1)} %get-tuple-element.117, bf16[1024,1024]{0,1:T(8,128)(2,1)S(1)} %get-tuple-element.115), kind=kOutput, calls=%fused_computation.26 | convolution fusion | flops 2177892352 | bytes 11542528 | tf_op jit(solution)/shard_map/dot_general | solution.py:29
  250.9 29.3 %collective-permute-done.11 = bf16[512,1024]{1,0:T(8,128)(2,1)S(1)} collective-permute-done((bf16[512,1024]{1,0:T(8,128)(2,1)S(1)}, bf16[512,1024]{1,0:T(8,128)(2,1)S(1)}, u32[]{:S(2)}, u32[]{:S(2)}) %collective-permute-start.11) | collective-permute-done | bytes 1048608 | tf_op jit(solution)/shard_map/ppermute | solution.py:21
  281.2 19.7 %collective-permute-done.9 = bf16[512,1024]{1,0:T(8,128)(2,1)S(1)} collective-permute-done((bf16[512,1024]{1,0:T(8,128)(2,1)S(1)}, bf16[512,1024]{1,0:T(8,128)(2,1)S(1)}, u32[]{:S(2)}, u32[]{:S(2)}) %collective-permute-start.9) | collective-permute-done | bytes 1048608 | tf_op jit(solution)/shard_map/ppermute | solution.py:21
  300.9 4.1 convert_reduce_fusion.7
  310.5 10.6 %attend_back_0.1.rest_0_ = f32[1024,768]{1,0:T(8,128)S(1)} custom-call(bf16[2048,768]{1,0:T(8,128)(2,1)S(1)} %add_convert_fusion.qkv_ref, bf16[1024,256]{1,0:T(8,128)(2,1)S(1)} %copy-done.4, bf16[1024,256]{1,0:T(8,128)(2,1)S(1)} %pad_maximum_fusion.18.grad_ref, f32[1024,256]{1,0:T(8,128)S(1)} %copy-done.8), custom_call_target="tpu_custom_call" | custom-call | tf_op jit(solution)/shard_map/attend_back_0/pallas_call | solution.py:227
  322.5 25.9 %attend_back_1024.1 = bf16[2048,768]{1,0:T(8,128)(2,1)S(1)} custom-call(bf16[2048,768]{1,0:T(8,128)(2,1)S(1)} %add_convert_fusion.qkv_ref, bf16[1024,256]{1,0:T(8,128)(2,1)S(1)} %copy-done.2, bf16[1024,256]{1,0:T(8,128)(2,1)S(1)} %pad_maximum_fusion.17.grad_ref, f32[1024,256]{1,0:T(8,128)S(1)} %copy-done.6, f32[1024,768]{1,0:T(8,128)S(1)} %attend_back_0.1.rest_0_), custom_call_target="tpu_custom_call" | custom-call | tf_op jit(solution)/shard_map/attend_back_1024/pallas_call | solution.py:227
  356.0 3.4 convolution_add_fusion
  364.1 5.3 convolution_convert_fusion.2
  369.5 2.6 reduce
  373.8 14.4 %collective-permute-done.16 = bf16[512,1024]{1,0:T(8,128)(2,1)} collective-permute-done((bf16[512,1024]{1,0:T(8,128)(2,1)}, bf16[512,1024]{1,0:T(8,128)(2,1)}, u32[]{:S(2)}, u32[]{:S(2)}) %collective-permute-start.16) | collective-permute-done | bytes 1048608 | tf_op jit(solution)/shard_map/ppermute | solution.py:21
  388.2 4.6 slice_reduce_fusion
  392.9 3.1 fusion.14
  396.0 4.3 copy.58
  400.6 4.7 fusion.39
  417.5 6.8 %copy.60 = bf16[1024,2048]{1,0:T(8,128)(2,1)} copy(bf16[1024,2048]{0,1:T(8,128)(2,1)} %pad_maximum_fusion.4) | data formatting | bytes 8388608
  424.3 3.6 add_convert_fusion.3
  427.9 39.8 %reduce-scatter.7.cloned.1.call-done = bf16[128,1152]{1,0:T(8,128)(2,1)} async-done(((bf16[1024,1152]{1,0:T(8,128)(2,1)}), bf16[128,1152]{1,0:T(8,128)(2,1)}) %reduce-scatter.7.cloned.1.call-update) | async-done | bytes 294928
  471.1 5.6 psum.7
  478.4 79.8 %reduce-scatter.9.cloned.1.call-done = bf16[128,2048]{1,0:T(8,128)(2,1)} async-done(((bf16[1024,2048]{1,0:T(8,128)(2,1)}), bf16[128,2048]{1,0:T(8,128)(2,1)}) %reduce-scatter.9.cloned.1.call-update) | async-done | bytes 524304
  (264 shorter events, 93.7 us)
Async XLA Ops:
  7.2 61.0 %all-gather.3.cloned.1.call-start = ((), (), s32[]{:S(2)}) async-start(), calls=%async_computation.2 | async-start | bytes 2654208 | tf_op jit(solution)/shard_map/all_gather | solution.py:299
  11.6 132.4 %all-gather.5.cloned.1.call-start = ((), (), s32[]{:S(2)}) async-start(), calls=%async_computation.3 | async-start | bytes 4718592 | tf_op jit(solution)/shard_map/all_gather | solution.py:301
  13.6 454.1 %reduce-scatter.7.cloned.1.call-start = ((), (), s32[]{:S(2)}) async-start(), calls=%async_computation.4 | async-start | bytes 2654208
  13.7 26.2 %collective-permute-start = (bf16[512,1024]{1,0:T(8,128)(2,1)S(1)}, bf16[512,1024]{1,0:T(8,128)(2,1)S(1)}, u32[]{:S(2)}, u32[]{:S(2)}) collective-permute-start(bf16[512,1024]{1,0:T(8,128)(2,1)S(1)} %copy-done.34), channel_id=1, source_target_pairs={{0,2},{2,0},{1,3},{3,1},{4,6},{6,4},{5,7},{7,5},{8,10},{10,8},{9,1... | collective-permute-start | bytes 3145736 | tf_op jit(solution)/shard_map/ppermute | solution.py:21
  16.7 25.8 %collective-permute-start.1 = (bf16[512,1024]{1,0:T(8,128)(2,1)S(1)}, bf16[512,1024]{1,0:T(8,128)(2,1)S(1)}, u32[]{:S(2)}, u32[]{:S(2)}) collective-permute-start(bf16[512,1024]{1,0:T(8,128)(2,1)S(1)} %copy-done.34), channel_id=1, source_target_pairs={{0,1},{1,0},{2,3},{3,2},{4,5},{5,4},{6,7},{7,6},{8,9},{9,8},{10,11... | collective-permute-start | bytes 3145736 | tf_op jit(solution)/shard_map/ppermute | solution.py:25
  39.8 2.8 collective-permute-start.2
  39.8 116.7 %collective-permute-start.10 = (bf16[512,1024]{1,0:T(8,128)(2,1)}, bf16[512,1024]{1,0:T(8,128)(2,1)}, u32[]{:S(2)}, u32[]{:S(2)}) collective-permute-start(bf16[512,1024]{1,0:T(8,128)(2,1)} %param.27), channel_id=1, source_target_pairs={{0,2},{2,0},{1,3},{3,1},{4,6},{6,4},{5,7},{7,5},{8,10},{10,8},{9,1... | collective-permute-start | bytes 3145736 | tf_op jit(solution)/shard_map/ppermute | solution.py:21
  68.2 79.8 %collective-permute-start.4 = (bf16[1024,1152]{0,1:T(8,128)(2,1)}, bf16[1024,1152]{0,1:T(8,128)(2,1)}, u32[]{:S(2)}, u32[]{:S(2)}) collective-permute-start(bf16[1024,1152]{0,1:T(8,128)(2,1)} %all-gather.3.cloned.1.call-done), channel_id=1, source_target_pairs={{0,1},{1,0},{2,3},{3,2},{4,5},{5,4},{6,7},{7,6},{8,9},{9,8},{10,11... | collective-permute-start | bytes 7077896 | tf_op jit(solution)/shard_map/ppermute | solution.py:25
  144.0 60.1 %collective-permute-start.8 = (bf16[1024,2048]{0,1:T(8,128)(2,1)}, bf16[1024,2048]{0,1:T(8,128)(2,1)S(1)}, u32[]{:S(2)}, u32[]{:S(2)}) collective-permute-start(bf16[1024,2048]{0,1:T(8,128)(2,1)} %all-gather.5.cloned.1.call-done), channel_id=1, source_target_pairs={{0,1},{1,0},{2,3},{3,2},{4,5},{5,4},{6,7},{7,6},{8,9},{9,8},{10,11... | collective-permute-start | bytes 12582920 | tf_op jit(solution)/shard_map/ppermute | solution.py:25
  145.1 6.5 %collective-permute-start.3 = (bf16[512,256]{1,0:T(8,128)(2,1)S(1)}, bf16[512,256]{1,0:T(8,128)(2,1)S(1)}, u32[]{:S(2)}, u32[]{:S(2)}) collective-permute-start(bf16[512,256]{1,0:T(8,128)(2,1)S(1)} %get-tuple-element.145), channel_id=1, source_target_pairs={{0,1},{1,0},{2,3},{3,2},{4,5},{5,4},{6,7},{7,6},{8,9},{9,8},{10,11... | collective-permute-start | bytes 786440 | tf_op jit(solution)/shard_map/ppermute | solution.py:25
  146.8 7.8 %collective-permute-start.6 = (bf16[512,256]{1,0:T(8,128)(2,1)S(1)}, bf16[512,256]{1,0:T(8,128)(2,1)S(1)}, u32[]{:S(2)}, u32[]{:S(2)}) collective-permute-start(bf16[512,256]{1,0:T(8,128)(2,1)S(1)} %get-tuple-element.147), channel_id=1, source_target_pairs={{0,1},{1,0},{2,3},{3,2},{4,5},{5,4},{6,7},{7,6},{8,9},{9,8},{10,11... | collective-permute-start | bytes 786440 | tf_op jit(solution)/shard_map/ppermute | solution.py:25
  153.0 26.1 %collective-permute-start.5 = (bf16[512,1024]{1,0:T(8,128)(2,1)S(1)}, bf16[512,1024]{1,0:T(8,128)(2,1)S(1)}, u32[]{:S(2)}, u32[]{:S(2)}) collective-permute-start(bf16[512,1024]{1,0:T(8,128)(2,1)S(1)} %convolution_convert_fusion.4), channel_id=1, source_target_pairs={{0,2},{2,0},{1,3},{3,1},{4,6},{6,4},{5,7},{7,5},{8,10},{10,8},{9,1... | collective-permute-start | bytes 3145736 | tf_op jit(solution)/shard_map/ppermute | solution.py:21
  156.0 44.8 %collective-permute-start.7 = (bf16[512,1024]{1,0:T(8,128)(2,1)S(1)}, bf16[512,1024]{1,0:T(8,128)(2,1)S(1)}, u32[]{:S(2)}, u32[]{:S(2)}) collective-permute-start(bf16[512,1024]{1,0:T(8,128)(2,1)S(1)} %convolution_convert_fusion.3), channel_id=1, source_target_pairs={{0,2},{2,0},{1,3},{3,1},{4,6},{6,4},{5,7},{7,5},{8,10},{10,8},{9,1... | collective-permute-start | bytes 3145736 | tf_op jit(solution)/shard_map/ppermute | solution.py:21
  159.1 141.9 %copy-start.24 = (bf16[512,1024]{1,0:T(8,128)(2,1)}, bf16[512,1024]{1,0:T(8,128)(2,1)S(1)}, u32[]{:S(2)}) copy-start(bf16[512,1024]{1,0:T(8,128)(2,1)S(1)} %get-tuple-element.105) | copy-start | bytes 3145732
  159.1 146.9 %copy-start.27 = (bf16[512,1024]{1,0:T(8,128)(2,1)}, bf16[512,1024]{1,0:T(8,128)(2,1)S(1)}, u32[]{:S(2)}) copy-start(bf16[512,1024]{1,0:T(8,128)(2,1)S(1)} %get-tuple-element.131) | copy-start | bytes 3145732
  159.9 40.9 %copy-start.10 = (bf16[512,1024]{1,0:T(8,128)(2,1)S(1)}, bf16[512,1024]{1,0:T(8,128)(2,1)}, u32[]{:S(2)}) copy-start(bf16[512,1024]{1,0:T(8,128)(2,1)} %copy-done.9) | copy-start | bytes 3145732
  159.9 40.8 %copy-start.13 = (bf16[512,1024]{1,0:T(8,128)(2,1)S(1)}, bf16[512,1024]{1,0:T(8,128)(2,1)}, u32[]{:S(2)}) copy-start(bf16[512,1024]{1,0:T(8,128)(2,1)} %copy-done.12) | copy-start | bytes 3145732
  219.3 27.7 %copy-start.51 = (bf16[512,2048]{1,0:T(8,128)(2,1)}, bf16[512,2048]{1,0:T(8,128)(2,1)S(1)}, u32[]{:S(2)}) copy-start(bf16[512,2048]{1,0:T(8,128)(2,1)S(1)} %get-tuple-element.159) | copy-start | bytes 6291460
  229.2 120.0 %copy-start.29 = (bf16[512,2048]{1,0:T(8,128)(2,1)}, bf16[512,2048]{1,0:T(8,128)(2,1)S(1)}, u32[]{:S(2)}) copy-start(bf16[512,2048]{1,0:T(8,128)(2,1)S(1)} %multiply_convert_fusion) | copy-start | bytes 6291460
  231.5 49.7 %collective-permute-start.12 = (bf16[512,1024]{1,0:T(8,128)(2,1)S(1)}, bf16[512,1024]{1,0:T(8,128)(2,1)S(1)}, u32[]{:S(2)}, u32[]{:S(2)}) collective-permute-start(bf16[512,1024]{1,0:T(8,128)(2,1)S(1)} %convolution_convert_fusion.5), channel_id=1, source_target_pairs={{0,2},{2,0},{1,3},{3,1},{4,6},{6,4},{5,7},{7,5},{8,10},{10,8},{9,1... | collective-permute-start | bytes 3145736 | tf_op jit(solution)/shard_map/ppermute | solution.py:21
  241.7 107.5 %copy-start.31 = (bf16[512,2048]{1,0:T(8,128)(2,1)}, bf16[512,2048]{1,0:T(8,128)(2,1)S(1)}, u32[]{:S(2)}) copy-start(bf16[512,2048]{1,0:T(8,128)(2,1)S(1)} %multiply_convert_fusion.1) | copy-start | bytes 6291460
  244.0 36.2 %collective-permute-start.11 = (bf16[512,1024]{1,0:T(8,128)(2,1)S(1)}, bf16[512,1024]{1,0:T(8,128)(2,1)S(1)}, u32[]{:S(2)}, u32[]{:S(2)}) collective-permute-start(bf16[512,1024]{1,0:T(8,128)(2,1)S(1)} %convolution_convert_fusion.6), channel_id=1, source_target_pairs={{0,2},{2,0},{1,3},{3,1},{4,6},{6,4},{5,7},{7,5},{8,10},{10,8},{9,1... | collective-permute-start | bytes 3145736 | tf_op jit(solution)/shard_map/ppermute | solution.py:21
  249.3 51.6 %collective-permute-start.9 = (bf16[512,1024]{1,0:T(8,128)(2,1)S(1)}, bf16[512,1024]{1,0:T(8,128)(2,1)S(1)}, u32[]{:S(2)}, u32[]{:S(2)}) collective-permute-start(bf16[512,1024]{1,0:T(8,128)(2,1)S(1)} %get-tuple-element.175), channel_id=1, source_target_pairs={{0,2},{2,0},{1,3},{3,1},{4,6},{6,4},{5,7},{7,5},{8,10},{10,8},{9,1... | collective-permute-start | bytes 3145736 | tf_op jit(solution)/shard_map/ppermute | solution.py:21
  305.9 3.8 collective-permute-start.14
  309.1 12.0 %collective-permute-start.13 = (bf16[512,256]{1,0:T(8,128)(2,1)S(1)}, bf16[512,256]{1,0:T(8,128)(2,1)S(1)}, u32[]{:S(2)}, u32[]{:S(2)}) collective-permute-start(bf16[512,256]{1,0:T(8,128)(2,1)S(1)} %slice.275), channel_id=1, source_target_pairs={{0,1},{1,0},{2,3},{3,2},{4,5},{5,4},{6,7},{7,6},{8,9},{9,8},{10,11... | collective-permute-start | bytes 786440 | tf_op jit(solution)/shard_map/ppermute | solution.py:25
  348.7 7.3 %collective-permute-start.15 = (bf16[1024,768]{1,0:T(8,128)(2,1)S(1)}, bf16[1024,768]{1,0:T(8,128)(2,1)S(1)}, u32[]{:S(2)}, u32[]{:S(2)}) collective-permute-start(bf16[1024,768]{1,0:T(8,128)(2,1)S(1)} %bitcast.93), channel_id=1, source_target_pairs={{0,1},{1,0},{2,3},{3,2},{4,5},{5,4},{6,7},{7,6},{8,9},{9,8},{10,11... | collective-permute-start | bytes 4718600 | tf_op jit(solution)/shard_map/ppermute | solution.py:25
  349.9 2.4 collective-permute-start.18
  353.7 18.7 %collective-permute-start.17 = (bf16[1024,256]{0,1:T(8,128)(2,1)S(1)}, bf16[1024,256]{0,1:T(8,128)(2,1)S(1)}, u32[]{:S(2)}, u32[]{:S(2)}) collective-permute-start(bf16[1024,256]{0,1:T(8,128)(2,1)S(1)} %slice.395), channel_id=1, source_target_pairs={{0,1},{1,0},{2,3},{3,2},{4,5},{5,4},{6,7},{7,6},{8,9},{9,8},{10,11... | collective-permute-start | bytes 1572872 | tf_op jit(solution)/shard_map/ppermute | solution.py:25
  362.6 25.5 %collective-permute-start.16 = (bf16[512,1024]{1,0:T(8,128)(2,1)}, bf16[512,1024]{1,0:T(8,128)(2,1)}, u32[]{:S(2)}, u32[]{:S(2)}) collective-permute-start(bf16[512,1024]{1,0:T(8,128)(2,1)} %select_convert_fusion), channel_id=1, source_target_pairs={{0,2},{2,0},{1,3},{3,1},{4,6},{6,4},{5,7},{7,5},{8,10},{10,8},{9,1... | collective-permute-start | bytes 3145736 | tf_op jit(solution)/shard_map/ppermute | solution.py:21
  400.3 157.9 %reduce-scatter.9.cloned.1.call-start = ((), (), s32[]{:S(2)}) async-start(), calls=%async_computation.5 | async-start | bytes 4718592
  405.3 4.2 collective-permute-start.19
  407.9 4.7 collective-permute-start.20
  (48 other events, 215.7 us)
Sparse Core Ops, SparseCore 0:
  11.7 56.4 all-gather.2
  70.8 73.1 all-gather.4
  400.4 67.2 reduce-scatter.6
  471.2 86.9 reduce-scatter.8
